TPU v7x, 128 devices: a whole 4x4x4 slice. The times are simulated.
128 devices in a mesh: user: 32 (over y, z, core), ctx: 4 (over x).
Axes of the slice: x: 4, y: 4, z: 4, core: 2. Of those that a mesh axis runs over, the one named last changes fastest.
Arguments:
- owner: int32 [32, 2048, 1], P('user', 'ctx'), may hold values from 0 to 127; in each aligned block of 512 rows (0 to 511, 512 to 1023, ..., all dimensions but the last counted through in order) at most 8 rows name the same one
- row: int32 [32, 2048], P('user', 'ctx'), may hold values from 0 to 2047
- lengths: int32 [32], P('user'), may hold values from 512 to 2048, as said below
- table: bfloat16 [262144, 512], P(('user', 'ctx')), may hold values from -36 to 36
- proj_weight: bfloat16 [512, 2048], replicated, may hold values from -0.25 to 0.25
- out_weight: bfloat16 [512, 512], replicated, may hold values from -0.25 to 0.25
- out_grad: bfloat16 [32, 2048, 512], P('user', 'ctx'), may hold values from -6 to 6
Outputs:
- mixed: bfloat16 [32, 2048, 512], P('user', 'ctx')
- table_grad: float32 [262144, 512], P(('user', 'ctx'))
Inputs may be any that keep to these rules, and one draw needn't show every extreme that they name: Among the events of one device (aligned blocks of 512 positions of one user) no owner is named more than 8 times, a bound that some block reaches. `lengths`: one user's history fills all 2048 positions and another's holds exactly 512 events.
All inputs are finite; a program needn't handle non-finite values.
Results may differ from a plain program's by a relative error of at most 0.007.
Values may be sent and summed in bfloat16 or wider, within the bound.
A program may use at most 128 MiB of HBM per device.

v0:
```python
import jax
import jax.numpy as jnp
from jax import lax
from jax.experimental import pallas as pl
from jax.experimental.pallas import tpu as pltpu
from jax.sharding import PartitionSpec as P

MESH = pl.DeviceIdType.MESH
F32 = jnp.float32
BF16 = jnp.bfloat16
NC = 4
ND = 128
TOK = 512
SEQ = 2048
D = 512
HD = 128
CAP = 8
ROWS = 2048
SLOTS = ND * CAP
GROUP = 32
EPSILON = 1e-05
SCALE = HD ** (-0.5)
QT = 256


def div(a, b):
    return lax.div(a, jnp.int32(b))


def rem(a, b):
    return lax.rem(a, jnp.int32(b))


def swapped(flat):
    core = rem(div(flat, 4), 2)
    x, y, z = rem(flat, 4), div(flat, 32), rem(div(flat, 8), 4)
    other = ((x * 4 + z) * 2 + core) * 4 + y
    return flat + core * (other - flat)


def place(flat):
    return (div(flat, NC), rem(flat, NC))


def iota(shape, axis):
    return lax.broadcasted_iota(jnp.int32, shape, axis)


def to_column(line):
    n = line.shape[1]
    eye = iota((n, n), 0) == iota((n, n), 1)
    return jnp.sum(jnp.where(eye, line, 0.0), axis=1, keepdims=True)


def to_line(column):
    n = column.shape[0]
    eye = iota((n, n), 0) == iota((n, n), 1)
    return jnp.sum(jnp.where(eye, column, 0.0), axis=0, keepdims=True)


def one_hot(match):
    return jnp.where(match, 1.0, 0.0).astype(BF16)


def dot(a, b, ca=1, cb=0):
    return lax.dot_general(a, b, (((ca,), (cb,)), ((), ())), preferred_element_type=F32)


def remote(src, dst, send, recv, target):
    return pltpu.make_async_remote_copy(
        src_ref=src, dst_ref=dst, send_sem=send, recv_sem=recv, device_id=target, device_id_type=MESH
    )


def tile_of(q, k):
    return div(q * (q + 1), 2) + k


def settle(view, sem):
    pltpu.make_async_copy(view, view, sem).wait()


def layer(
    owner, row, length, table_h, pw_h, ow_h, og_h,
    mixed, recv2, wrow,
    table, pw, ow, og, og_in, wh, vbuf, vall, out1, recv1, x_all, emb, normed, r_x,
    q_s, k_s, v_s, g_s, slopes, gg_send, gg, att, w_t, d_t, d_att, dq_s, gated_s, dg_s, dk_s, dv_s, dqo_s,
    gated_r, pg, mix, stats, out2, d_kv,
    load, ids_s, ids_r, og_s, og_r, a_s, a_r, gg_ss, gg_rs, x_ss, x_rs, st_s, st_r, ex_s, ex_r, mx_s, mx_r, b_s, b_r,
):
    user, ctx = lax.axis_index("user"), lax.axis_index("ctx")
    me = user * NC + ctx
    core = rem(user, 2)
    held = swapped(me)
    block = rem(held, NC)
    away = held != me

    def peer(j):
        z = rem(div(user, 2), 4)
        other = (j * 4 + z) * 2 + 1
        return (user + core * (other - user), j + core * (ctx - j))

    def each_peer(k):
        return rem(block + k, NC)

    barrier = pltpu.get_barrier_semaphore()

    def greet(k, carry):
        pl.semaphore_signal(barrier, inc=1, device_id=place(rem(me + k, ND)), device_id_type=MESH)
        return carry

    lax.fori_loop(1, ND, greet, 0)

    head = pl.multiple_of(block * HD, HD)
    loads = [
        pltpu.make_async_copy(og_h, og_in, load.at[0]),
        pltpu.make_async_copy(table_h, table, load.at[1]),
        pltpu.make_async_copy(ow_h, ow, load.at[2]),
        pltpu.make_async_copy(pw_h, pw, load.at[3]),
    ]
    for copy in loads:
        copy.start()

    places = ctx * TOK + iota((1, TOK), 1)
    valid = places < length[0]
    own = jnp.where(valid, owner[...], -1)
    match = iota((ND, TOK), 0) == own
    before = one_hot(iota((TOK, TOK), 0) < iota((TOK, TOK), 1))
    rank = dot(one_hot(match), before)
    slot = jnp.sum(jnp.where(match, rank, 0.0), axis=0, keepdims=True).astype(jnp.int32)
    packed = jnp.where(valid, (own * CAP + slot) * ROWS + row[...], -1)
    vbuf[0] = packed
    vall[me] = packed

    pl.semaphore_wait(barrier, ND - 1)

    def tell(k, carry):
        remote(vbuf.at[0], vall.at[me], ids_s, ids_r, place(rem(me + k, ND))).start()
        return carry

    lax.fori_loop(1, ND, tell, 0)
    loads[0].wait()

    @pl.when(away)
    def _():
        remote(og_in, og, og_s, og_r, place(held)).start()

    settle(vall.at[pl.ds(0, ND - 1)], ids_r)
    loads[1].wait()

    def answer(step, carry):
        group = rem(step + div(me, GROUP), ND // GROUP)
        first = pl.multiple_of(group * GROUP, GROUP)
        asked = vall[pl.ds(first, GROUP)]
        mine = (lax.shift_right_arithmetic(asked, 11) - me * CAP) == iota((GROUP, CAP, 1), 1)
        wanted = jnp.where(mine, (jnp.bitwise_and(asked, ROWS - 1) + 1).astype(F32), 0.0)
        wanted = (jnp.sum(wanted, axis=2, keepdims=True) - 1.0).reshape(GROUP * CAP, 1)
        wrow[:, pl.ds(pl.multiple_of(group * GROUP * CAP, GROUP * CAP), GROUP * CAP)] = to_line(wanted)
        found = dot(one_hot(iota((GROUP * CAP, ROWS), 1) == wanted.astype(jnp.int32)), table[...])
        halves = [found[:, :256].reshape(GROUP, CAP, 256), found[:, 256:].reshape(GROUP, CAP, 256)]
        out1[pl.ds(first, GROUP)] = jnp.concatenate(halves, axis=1).astype(BF16)

        def send(k, inner):
            source = first + rem(k + me, GROUP)
            target = swapped(source)

            @pl.when(target != me)
            def _():
                remote(out1.at[source], recv1.at[me], a_s, a_r, place(target)).start()

            @pl.when(target == me)
            def _():
                recv1[me] = out1[source]

            return inner

        lax.fori_loop(0, GROUP, send, 0)
        return carry

    lax.fori_loop(0, ND // GROUP, answer, 0)

    slot_line = lax.shift_right_arithmetic(vall[held], 11).astype(F32)
    slot_col = to_column(slot_line)
    inside = slot_col >= 0.0
    loads[2].wait()
    loads[3].wait()

    @pl.when(away)
    def _():
        settle(og, og_r)

    @pl.when(jnp.logical_not(away))
    def _():
        og[...] = og_in[...]

    masked = jnp.where(inside, og[...], jnp.zeros((TOK, D), BF16))
    og[...] = masked
    gated_grad = dot(masked, ow[...], 1, 1).astype(BF16)
    for j in range(NC):
        gg_send[j] = gated_grad[:, j * HD:(j + 1) * HD]
    for k in range(1, NC):
        j = each_peer(k)
        remote(gg_send.at[j], gg.at[block], gg_ss, gg_rs, peer(j)).start()
    gg[block] = gg_send[block]
    for part in range(4):
        wh[:, part * HD:(part + 1) * HD] = pw[:, pl.ds(pl.multiple_of(part * D + head, HD), HD)]

    settle(recv1.at[pl.ds(0, ND - 1)], a_r)
    embed = jnp.zeros((TOK, D), F32)
    for g in range(ND // GROUP):
        got = recv1[g * GROUP:(g + 1) * GROUP].astype(F32)
        rows = jnp.concatenate(
            [got[:, :CAP].reshape(GROUP * CAP, 256), got[:, CAP:].reshape(GROUP * CAP, 256)], axis=1
        ).astype(BF16)
        lanes = iota((TOK, GROUP * CAP), 1) + g * GROUP * CAP
        embed = embed + dot(one_hot(lanes == slot_col.astype(jnp.int32)), rows)
    emb[...] = embed.astype(BF16)
    center = jnp.mean(embed, -1, keepdims=True)
    deviation = embed - center
    inverse = lax.rsqrt(jnp.mean(deviation * deviation, -1, keepdims=True) + EPSILON)
    norm = deviation * inverse
    normed[...] = norm
    r_x[...] = inverse
    x_all[block] = norm.astype(BF16)
    for k in range(1, NC):
        remote(x_all.at[block], x_all.at[block], x_ss.at[k], x_rs.at[k], peer(each_peer(k))).start()

    def project(j):
        for half in range(2):
            projected = dot(x_all[j, half * 256:(half + 1) * 256], wh[...])
            sigma = jax.nn.sigmoid(projected)
            silu = projected * sigma
            where = pl.ds(pl.multiple_of(j * TOK + half * 256, 256), 256)
            slopes[where, :] = sigma + silu * (1.0 - sigma)
            low = silu.astype(BF16)
            g_s[where, :] = low[:, :HD]
            q_s[where, :] = low[:, HD:2 * HD]
            k_s[where, :] = low[:, 2 * HD:3 * HD]
            v_s[where, :] = low[:, 3 * HD:]

    project(block)
    for k in range(1, NC):
        settle(x_all.at[0], x_rs.at[k])
        project(rem(block - k + NC, NC))
    settle(gg.at[pl.ds(0, 3)], gg_rs)

    def forward(qb, carry):
        rows = pl.ds(pl.multiple_of(qb * QT, QT), QT)
        query = q_s[rows, :]

        def tile(kb, total):
            cols = pl.ds(pl.multiple_of(kb * TOK, TOK), TOK)
            scores = dot(query, k_s[cols, :], 1, 1) * SCALE
            allowed = (iota((QT, TOK), 1) - iota((QT, TOK), 0)) <= (qb * QT - kb * TOK)
            sigma = jax.nn.sigmoid(scores)
            silu = scores * sigma
            weights = jnp.where(allowed, silu, 0.0).astype(BF16)
            place_t = tile_of(div(qb, 2), kb)
            half = pl.ds(pl.multiple_of(rem(qb, 2) * QT, QT), QT)
            w_t[place_t, half, :] = weights
            d_t[place_t, half, :] = jnp.where(allowed, (sigma + silu * (1.0 - sigma)) * SCALE, 0.0)
            return total + dot(weights, v_s[cols, :])

        total = lax.fori_loop(0, div(qb, 2) + 1, tile, jnp.zeros((QT, HD), F32))
        att[rows, :] = total
        gate = g_s[rows, :].astype(F32)
        incoming = gg[div(qb, 2), pl.ds(pl.multiple_of(rem(qb, 2) * QT, QT), QT), :].astype(F32)
        cot = incoming * gate
        mean = jnp.mean(total, -1, keepdims=True)
        off = total - mean
        spread = jnp.sum(off * off, -1, keepdims=True)
        c_sum = jnp.sum(cot, -1, keepdims=True)
        c_off = jnp.sum(cot * off, -1, keepdims=True)
        lane = iota((QT, HD), 1)
        table4 = jnp.where(lane == 0, mean, jnp.where(lane == 1, spread, jnp.where(lane == 2, c_sum, c_off)))
        stats[block, :, rows] = table4.T[:8]
        return carry

    lax.fori_loop(0, SEQ // QT, forward, 0)
    for k in range(1, NC):
        remote(stats.at[block], stats.at[block], st_s, st_r, peer(each_peer(k))).start()
    settle(stats.at[pl.ds(0, 3)], st_r)

    means = [stats[h, 0:1, :] for h in range(NC)]
    mean = (means[0] + means[1] + means[2] + means[3]) * (1.0 / NC)
    spread = 0.0
    c_sum = 0.0
    c_off = 0.0
    for h in range(NC):
        gap = means[h] - mean
        spread = spread + stats[h, 1:2, :] + HD * gap * gap
        c_sum = c_sum + stats[h, 2:3, :]
        c_off = c_off + stats[h, 3:4, :] + stats[h, 2:3, :] * gap
    r_a = lax.rsqrt(spread * (1.0 / D) + EPSILON)
    c_mean = c_sum * (1.0 / D)
    c_norm = r_a * c_off * (1.0 / D)
    sub = iota((8, SEQ), 0)
    rows8 = jnp.where(sub == 0, mean, jnp.where(sub == 1, r_a, jnp.where(sub == 2, c_mean, c_norm)))

    for b in range(NC):
        wide = jnp.concatenate([rows8[:, b * TOK:(b + 1) * TOK]] * 16, axis=0).T
        at = slice(b * TOK, (b + 1) * TOK)
        a_norm = (att[at, :] - wide[:, 0:1]) * wide[:, 1:2]
        gate = g_s[at, :].astype(F32)
        incoming = gg[b].astype(F32)
        cot = incoming * gate
        gated_s[b] = (a_norm * gate).astype(BF16)
        dg_s[b] = (incoming * a_norm * slopes[at, :HD]).astype(BF16)
        d_att[at, :] = (wide[:, 1:2] * (cot - wide[:, 2:3] - a_norm * wide[:, 3:4])).astype(BF16)
    for k in range(1, NC):
        j = each_peer(k)
        remote(gated_s.at[j], gated_r.at[:, pl.ds(head, HD)], ex_s.at[0], ex_r.at[0], peer(j)).start()
        remote(dg_s.at[j], pg.at[:, pl.ds(head, HD)], ex_s.at[1], ex_r.at[1], peer(j)).start()
    gated_r[:, pl.ds(head, HD)] = gated_s[block]
    pg[:, pl.ds(head, HD)] = dg_s[block]

    dq_s[...] = jnp.zeros((SEQ, HD), F32)

    def backward(step, carry):
        kb = rem(block + 1 + step, NC)
        cols = pl.ds(pl.multiple_of(kb * TOK, TOK), TOK)
        d_kv[...] = jnp.zeros((TOK, 2 * HD), F32)

        def tile(qb, inner):
            rows = pl.ds(pl.multiple_of(qb * TOK, TOK), TOK)
            da = d_att[rows, :]
            slope = dot(da, v_s[cols, :], 1, 1)
            ds = (slope * d_t[tile_of(qb, kb)]).astype(BF16)
            dq_s[rows, :] += dot(ds, k_s[cols, :])
            d_kv[:, :HD] += dot(ds, q_s[rows, :], 0, 0)
            d_kv[:, HD:] += dot(w_t[tile_of(qb, kb)], da, 0, 0)
            return inner

        lax.fori_loop(kb, NC, tile, 0)
        both = (d_kv[...] * slopes[cols, 2 * HD:]).astype(BF16)
        dk_s[kb] = both[:, :HD]
        dv_s[kb] = both[:, HD:]

        @pl.when(kb != block)
        def _():
            remote(dk_s.at[kb], pg.at[:, pl.ds(2 * D + head, HD)], ex_s.at[2], ex_r.at[2], peer(kb)).start()
            remote(dv_s.at[kb], pg.at[:, pl.ds(3 * D + head, HD)], ex_s.at[3], ex_r.at[3], peer(kb)).start()

        return carry

    lax.fori_loop(0, NC, backward, 0)
    for b in range(NC):
        at = slice(b * TOK, (b + 1) * TOK)
        dqo_s[b] = (dq_s[at, :] * slopes[at, HD:2 * HD]).astype(BF16)
    for k in range(1, NC):
        j = each_peer(k)
        remote(dqo_s.at[j], pg.at[:, pl.ds(D + head, HD)], ex_s.at[4], ex_r.at[4], peer(j)).start()
    pg[:, pl.ds(D + head, HD)] = dqo_s[block]
    pg[:, pl.ds(2 * D + head, HD)] = dk_s[block]
    pg[:, pl.ds(3 * D + head, HD)] = dv_s[block]

    settle(gated_r.at[:, pl.ds(0, 3 * HD)], ex_r.at[0])
    mix[...] = (emb[...].astype(F32) + dot(gated_r[...], ow[...])).astype(BF16)

    @pl.when(away)
    def _():
        remote(mix, mixed, mx_s, mx_r, place(held)).start()

    @pl.when(jnp.logical_not(away))
    def _():
        mixed[...] = mix[...]

    for kind in range(1, 5):
        settle(pg.at[:, pl.ds(0, 3 * HD)], ex_r.at[kind])
    incoming = dot(pg[...], pw[...], 1, 1)
    norm = normed[...]
    embed_grad = r_x[...] * (
        incoming
        - jnp.mean(incoming, -1, keepdims=True)
        - norm * jnp.mean(incoming * norm, -1, keepdims=True)
    ) + og[...].astype(F32)
    embed_grad = embed_grad.astype(BF16)

    for step in range(ND // GROUP):
        group = rem(step + div(me, GROUP), ND // GROUP)
        first = pl.multiple_of(group * GROUP, GROUP)
        slots = iota((GROUP * CAP, TOK), 0) + group * (GROUP * CAP)
        sorted_rows = dot(one_hot(slots == slot_line.astype(jnp.int32)), embed_grad)
        halves = [sorted_rows[:, :256].reshape(GROUP, CAP, 256), sorted_rows[:, 256:].reshape(GROUP, CAP, 256)]
        out2[pl.ds(first, GROUP)] = jnp.concatenate(halves, axis=1).astype(BF16)

        def send(k, inner):
            target = first + rem(k + me, GROUP)

            @pl.when(target != me)
            def _():
                remote(out2.at[target], recv2.at[held], b_s, b_r, place(target)).start()

            @pl.when(target == me)
            def _():
                recv2[held] = out2[target]

            return inner

        lax.fori_loop(0, GROUP, send, 0)

    settle(vall.at[pl.ds(0, ND - 1)], ids_s)
    settle(out1.at[pl.ds(0, ND - 1)], a_s)
    settle(gg_send.at[pl.ds(0, 3)], gg_ss)
    for k in range(1, NC):
        settle(x_all.at[0], x_ss.at[k])
    settle(stats.at[pl.ds(0, 3)], st_s)
    for kind in range(5):
        settle(pg.at[:, pl.ds(0, 3 * HD)], ex_s.at[kind])

    @pl.when(away)
    def _():
        settle(og_in, og_s)
        settle(mix, mx_s)
        settle(mixed, mx_r)

    settle(out2.at[pl.ds(0, ND - 1)], b_s)
    settle(recv2.at[pl.ds(0, ND - 1)], b_r)


def scatter_kernel(wrow, recv2, out, rows):
    step = pl.program_id(0)

    @pl.when(step == 0)
    def _():
        for g in range(ND // GROUP):
            got = recv2[g * GROUP:(g + 1) * GROUP].astype(F32)
            rows[g * GROUP * CAP:(g + 1) * GROUP * CAP] = jnp.concatenate(
                [got[:, :CAP].reshape(GROUP * CAP, 256), got[:, CAP:].reshape(GROUP * CAP, 256)], axis=1
            ).astype(BF16)

    size = out.shape[0]
    wanted = wrow[...].astype(jnp.int32)
    out[...] = dot(one_hot((iota((size, SLOTS), 0) + step * size) == wanted), rows[...])


def shards(owner, row, lengths, table, proj_weight, out_weight, out_grad):
    vmem = pl.BlockSpec(memory_space=pltpu.VMEM)
    hbm = pl.BlockSpec(memory_space=pl.ANY)
    V = pltpu.VMEM
    DMA = pltpu.SemaphoreType.DMA
    mixed, recv2, wrow = pl.pallas_call(
        layer,
        out_shape=(
            jax.ShapeDtypeStruct((TOK, D), BF16),
            jax.ShapeDtypeStruct((ND, 2 * CAP, 256), BF16),
            jax.ShapeDtypeStruct((1, SLOTS), F32),
        ),
        in_specs=[vmem, vmem, pl.BlockSpec(memory_space=pltpu.SMEM), hbm, hbm, hbm, hbm],
        out_specs=(vmem, vmem, vmem),
        scratch_shapes=[
            V((ROWS, D), BF16), V((D, 4 * D), BF16), V((D, D), BF16), V((TOK, D), BF16), V((TOK, D), BF16),
            V((D, 4 * HD), BF16), V((1, 1, TOK), jnp.int32), V((ND, 1, TOK), jnp.int32),
            V((ND, 2 * CAP, 256), BF16), V((ND, 2 * CAP, 256), BF16), V((NC, TOK, D), BF16), V((TOK, D), BF16),
            V((TOK, D), F32), V((TOK, 1), F32),
            V((SEQ, HD), BF16), V((SEQ, HD), BF16), V((SEQ, HD), BF16), V((SEQ, HD), BF16), V((SEQ, 4 * HD), F32),
            V((NC, TOK, HD), BF16), V((NC, TOK, HD), BF16), V((SEQ, HD), F32), V((10, TOK, TOK), BF16), V((10, TOK, TOK), F32),
            V((SEQ, HD), BF16), V((SEQ, HD), F32),
            V((NC, TOK, HD), BF16), V((NC, TOK, HD), BF16), V((NC, TOK, HD), BF16), V((NC, TOK, HD), BF16),
            V((NC, TOK, HD), BF16),
            V((TOK, D), BF16), V((TOK, 4 * D), BF16), V((TOK, D), BF16), V((NC, 8, SEQ), F32),
            V((ND, 2 * CAP, 256), BF16), V((TOK, 2 * HD), F32),
            DMA((4,)), DMA, DMA, DMA, DMA, DMA, DMA, DMA, DMA, DMA((NC,)), DMA((NC,)), DMA, DMA,
            DMA((5,)), DMA((5,)), DMA, DMA, DMA, DMA,
        ],
        compiler_params=pltpu.CompilerParams(
            collective_id=0, has_side_effects=True, vmem_limit_bytes=52 * 1024 * 1024
        ),
    )(
        owner.reshape(1, TOK), row.reshape(1, TOK), lengths, table, proj_weight, out_weight,
        out_grad.reshape(TOK, D),
    )
    size = 256
    table_grad = pl.pallas_call(
        scatter_kernel,
        grid=(ROWS // size,),
        out_shape=jax.ShapeDtypeStruct((ROWS, D), F32),
        in_specs=[
            pl.BlockSpec((1, SLOTS), lambda i: (0, 0)),
            pl.BlockSpec((ND, 2 * CAP, 256), lambda i: (0, 0, 0)),
        ],
        out_specs=pl.BlockSpec((size, D), lambda i: (i, 0)),
        scratch_shapes=[V((SLOTS, D), BF16)],
        compiler_params=pltpu.CompilerParams(vmem_limit_bytes=32 * 1024 * 1024),
    )(wrow, recv2)
    return (mixed.reshape(1, TOK, D), table_grad)


def solution(mesh):
    placed = (
        P("user", "ctx", None),
        P("user", "ctx"),
        P("user"),
        P(("user", "ctx"), None),
        P(),
        P(),
        P("user", "ctx", None),
    )
    return jax.shard_map(
        shards,
        mesh=mesh,
        in_specs=placed,
        out_specs=(P("user", "ctx", None), P(("user", "ctx"), None)),
        check_vma=False,
    )
```

profile of v0, /device:TPU:1, one launch (start us, length us, event | category | flops | bytes accessed | tf_op | source)
XLA Modules:
  0.0 145.8 jit_solution(15844440276483494891)
XLA Ops:
  1.3 0.0 copy-start.1
  1.3 1.0 copy-done.1
  2.3 0.0 copy-start.2
  2.3 1.0 copy-done.2
  3.4 0.0 copy-start.3
  3.4 0.7 copy-done.3
  4.0 0.0 copy-start.4
  4.0 0.7 copy-done.4
  4.7 133.6 %shard_map.86 = (bf16[512,512]{1,0:T(8,128)(2,1)S(1)}, bf16[128,16,256]{2,1,0:T(8,128)(2,1)}, f32[1,1024]{1,0:T(1,128)S(1)}) custom-call(s32[1,512]{1,0:T(1,128)S(1)} %bitcast.5, s32[1,512]{1,0:T(1,128)S(1)} %copy-done.4, s32[1]{0:T(128)S(6)} %copy.10.length, bf16[2048,512]{1,0:T(8,128)(2,1)} %table_h.1, bf16[512,2048]{1,0:T(8,128)(2,1)} %pw_h.1, ...), custom_call_target="tpu_custom_call" | custom-call | tf_op jit(solution)/shard_map/pallas_call | solution.py:442
  138.3 0.0 copy-start
  138.3 1.2 copy-done
  139.5 5.4 %shard_map.87 = f32[2048,512]{1,0:T(8,128)} custom-call(f32[1,1024]{1,0:T(1,128)S(1)} %get-tuple-element.6.wrow, bf16[128,16,256]{2,1,0:T(8,128)(2,1)S(1)} %copy-done), custom_call_target="tpu_custom_call" | custom-call | tf_op jit(solution)/shard_map/pallas_call | solution.py:474
  145.0 0.8 copy.11
Async XLA Ops:
  1.3 1.0 copy-start.1
  2.3 1.0 copy-start.2
  3.4 0.7 copy-start.3
  4.0 0.7 copy-start.4
  138.3 1.2 copy-start
where the time goes:
time: 146 us
  Pallas kernels  139 us (95%)
  local copies, waits for them, and re-layouts  5.45 us (4%)
    pallas_call x1, Pallas kernels, shards(): pl.pallas_call(layer, out_shape=(jax.ShapeDtypeStruct((TOK, D), BF16), ja...  134 us
    unnamed x11, local copies, waits for them, and re-layouts  5.45 us
    pallas_call x1, Pallas kernels, shards(): pl.pallas_call(scatter_kernel, grid=(ROWS // size,), out_shape=jax.ShapeD...  5.44 us

commit v1 on v0

v1 whole, which is shorter than its diff:
```python
import jax
import jax.numpy as jnp
from jax import lax
from jax.experimental import pallas as pl
from jax.experimental.pallas import tpu as pltpu
from jax.sharding import PartitionSpec as P

MESH = pl.DeviceIdType.MESH
F32 = jnp.float32
BF16 = jnp.bfloat16
NC = 4
ND = 128
TOK = 512
SEQ = 2048
D = 512
HD = 128
CAP = 8
ROWS = 2048
SLOTS = ND * CAP
GROUP = 32
EPSILON = 1e-05
SCALE = HD ** (-0.5)
QT = 256
UNROLL = 16


def div(a, b):
    return lax.div(a, jnp.int32(b))


def rem(a, b):
    return lax.rem(a, jnp.int32(b))


def number_at(x, y, z, core):
    return ((rem(x + y + z, 4) * 4 + z) * 2 + core) * 4 + x


def coords(number):
    x, core, z = rem(number, 4), rem(div(number, 4), 2), rem(div(number, 8), 4)
    return x, rem(div(number, 32) + 8 - x - z, 4), z, core


def worker(number):
    x, y, z, core = coords(number)
    return number_at(x + core * (y - x), y + core * (rem(x + y, 4) - y), z, core)


def holder(number):
    x, y, z, core = coords(number)
    return number_at(x + core * (rem(y + 4 - x, 4) - x), y + core * (x - y), z, core)


def place(number):
    x, y, z, core = coords(number)
    return ((y * 4 + z) * 2 + core, x)


def iota(shape, axis):
    return lax.broadcasted_iota(jnp.int32, shape, axis)


def to_column(line):
    n = line.shape[1]
    eye = iota((n, n), 0) == iota((n, n), 1)
    return jnp.sum(jnp.where(eye, line, 0.0), axis=1, keepdims=True)


def to_line(column):
    n = column.shape[0]
    eye = iota((n, n), 0) == iota((n, n), 1)
    return jnp.sum(jnp.where(eye, column, 0.0), axis=0, keepdims=True)


def one_hot(match):
    return jnp.where(match, 1.0, 0.0).astype(BF16)


def dot(a, b, ca=1, cb=0):
    return lax.dot_general(a, b, (((ca,), (cb,)), ((), ())), preferred_element_type=F32)


def others(act, width=UNROLL):
    whole = (ND - 1) // width

    def some(step, carry):
        for k in range(width):
            act(step * width + (k + 1))
        return carry

    lax.fori_loop(0, whole, some, 0)
    for k in range(whole * width + 1, ND):
        act(jnp.int32(k))


def members(act, width=UNROLL):
    def some(step, carry):
        for k in range(width):
            act(step * width + k)
        return carry

    lax.fori_loop(0, GROUP // width, some, 0)


def remote(src, dst, send, recv, target):
    return pltpu.make_async_remote_copy(
        src_ref=src, dst_ref=dst, send_sem=send, recv_sem=recv, device_id=target, device_id_type=MESH
    )


def tile_of(q, k):
    return div(q * (q + 1), 2) + k


def settle(view, sem):
    pltpu.make_async_copy(view, view, sem).wait()


def silu_parts(values):
    half = values * 0.5
    t = jnp.tanh(half)
    turned = half * t
    return half + turned, (0.5 + 0.5 * t) * (1.0 + (half - turned))


def layer(
    owner, row, length, table_h, pw_h, ow_h, og_h,
    mixed, recv2, wrow,
    table, pw, ow, og, og_in, og_mid, vbuf, vall, out1, recv1, emb, normed, r_x, slopes, gate_s, gg,
    out_q, out_k, out_v, out_c, out_an, out_dk, out_dv, out_dq, q_s, k_s, v_s, c_s, an_s, dqkv,
    att, w_t, d_t, d_att, d_att_t, q_t, dq_acc, d_kv, e_acc, mix, stats, out2,
    load, ids_s, ids_r, og_s, og_r, a_s, a_r, st_s, st_r, ex_s, ex_r, mx_s, mx_r, b_s, b_r,
):
    user, ctx = lax.axis_index("user"), lax.axis_index("ctx")
    core, z_at, y_at = rem(user, 2), rem(div(user, 2), 4), div(user, 8)
    me = number_at(ctx, y_at, z_at, core)
    held = holder(me)
    relay = number_at(ctx, y_at + core * (rem(ctx + y_at, 4) - y_at), z_at, core)
    beyond = number_at(ctx + core * (rem(y_at + 4 - ctx, 4) - ctx), y_at, z_at, core)
    block = rem(held, NC)
    away = held != me

    def peer(j):
        other = (rem(j + ctx, 4) * 4 + z_at) * 2 + 1
        return (user + core * (other - user), j + core * (ctx - j))

    def each_peer(k):
        return rem(block + k, NC)

    barrier = pltpu.get_barrier_semaphore()

    def greet(k):
        pl.semaphore_signal(barrier, inc=1, device_id=place(rem(me + k, ND)), device_id_type=MESH)

    others(greet)

    head = pl.multiple_of(block * HD, HD)
    loads = [
        pltpu.make_async_copy(og_h, og_in, load.at[0]),
        pltpu.make_async_copy(table_h, table, load.at[1]),
        pltpu.make_async_copy(ow_h, ow, load.at[2]),
        pltpu.make_async_copy(pw_h, pw, load.at[3]),
    ]
    for copy in loads:
        copy.start()

    places = ctx * TOK + iota((1, TOK), 1)
    valid = places < length[0]
    own_x, own_y = jnp.bitwise_and(owner[...], 3), lax.shift_right_logical(owner[...], 5)
    own_z = jnp.bitwise_and(lax.shift_right_logical(owner[...], 3), 3)
    own_w = jnp.bitwise_and(own_x + own_y + own_z, 3)
    own = jnp.where(valid, jnp.bitwise_and(owner[...], 31) + own_w * 32, -1)
    match = iota((ND, TOK), 0) == own
    before = one_hot(iota((TOK, TOK), 0) < iota((TOK, TOK), 1))
    rank = dot(one_hot(match), before)
    slot = jnp.sum(jnp.where(match, rank, 0.0), axis=0, keepdims=True).astype(jnp.int32)
    packed = jnp.where(valid, (own * CAP + slot) * ROWS + row[...], -1)
    vbuf[0] = packed
    vall[me] = packed

    pl.semaphore_wait(barrier, ND - 1)

    def tell(k):
        remote(vbuf.at[0], vall.at[me], ids_s, ids_r, place(rem(me + k, ND))).start()

    loads[0].wait()

    @pl.when(relay != me)
    def _():
        remote(og_in, og_mid, og_s.at[0], og_r.at[0], place(relay)).start()

    @pl.when(relay == me)
    def _():
        og_mid[...] = og_in[...]

    others(tell)
    settle(vall.at[pl.ds(0, ND - 1)], ids_r)

    @pl.when(relay != me)
    def _():
        settle(og_mid, og_r.at[0])

    @pl.when(beyond != me)
    def _():
        remote(og_mid, og, og_s.at[1], og_r.at[1], place(beyond)).start()

    loads[1].wait()

    def answer(step, carry):
        group = rem(step + div(me, GROUP), ND // GROUP)
        first = pl.multiple_of(group * GROUP, GROUP)
        asked = vall[pl.ds(first, GROUP)]
        mine = (lax.shift_right_arithmetic(asked, 11) - me * CAP) == iota((GROUP, CAP, 1), 1)
        wanted = jnp.where(mine, (jnp.bitwise_and(asked, ROWS - 1) + 1).astype(F32), 0.0)
        wanted = (jnp.sum(wanted, axis=2, keepdims=True) - 1.0).reshape(GROUP * CAP, 1)
        wrow[:, pl.ds(pl.multiple_of(group * GROUP * CAP, GROUP * CAP), GROUP * CAP)] = to_line(wanted)
        found = dot(one_hot(iota((GROUP * CAP, ROWS), 1) == wanted.astype(jnp.int32)), table[...])
        halves = [found[:, :256].reshape(GROUP, CAP, 256), found[:, 256:].reshape(GROUP, CAP, 256)]
        out1[pl.ds(first, GROUP)] = jnp.concatenate(halves, axis=1).astype(BF16)

        def send(k):
            source = first + rem(k + me, GROUP)
            target = worker(source)

            @pl.when(target != me)
            def _():
                remote(out1.at[source], recv1.at[me], a_s, a_r, place(target)).start()

            @pl.when(target == me)
            def _():
                recv1[me] = out1[source]

        members(send)
        return carry

    lax.fori_loop(0, ND // GROUP, answer, 0)

    slot_line = lax.shift_right_arithmetic(vall[held], 11).astype(F32)
    slot_col = to_column(slot_line)
    loads[2].wait()
    loads[3].wait()

    @pl.when(beyond != me)
    def _():
        settle(og, og_r.at[1])

    @pl.when(beyond == me)
    def _():
        og[...] = og_mid[...]

    masked = jnp.where(slot_col >= 0.0, og[...], jnp.zeros((TOK, D), BF16))
    og[...] = masked
    gg[...] = dot(masked, ow[...], 1, 1)

    settle(recv1.at[pl.ds(0, ND - 1)], a_r)
    embed = jnp.zeros((TOK, D), F32)
    for g in range(ND // GROUP):
        got = recv1[g * GROUP:(g + 1) * GROUP].astype(F32)
        rows = jnp.concatenate(
            [got[:, :CAP].reshape(GROUP * CAP, 256), got[:, CAP:].reshape(GROUP * CAP, 256)], axis=1
        ).astype(BF16)
        lanes = iota((TOK, GROUP * CAP), 1) + g * GROUP * CAP
        embed = embed + dot(one_hot(lanes == slot_col.astype(jnp.int32)), rows)
    emb[...] = embed.astype(BF16)
    center = jnp.mean(embed, -1, keepdims=True)
    deviation = embed - center
    inverse = lax.rsqrt(jnp.mean(deviation * deviation, -1, keepdims=True) + EPSILON)
    norm = deviation * inverse
    normed[...] = norm
    r_x[...] = inverse
    norm_low = norm.astype(BF16)

    def spread(low, outbox, inbox, kind):
        for j in range(NC):
            outbox[j] = low[:, j * HD:(j + 1) * HD]
        for k in range(1, NC):
            j = each_peer(k)
            remote(outbox.at[j], inbox.at[block], ex_s.at[kind], ex_r.at[kind], peer(j)).start()
        inbox[block] = outbox[block]

    for kind, (outbox, inbox) in enumerate(((out_q, q_s), (out_k, k_s), (out_v, v_s))):
        part = slice((kind + 1) * D, (kind + 2) * D)
        silu, slope = silu_parts(dot(norm_low, pw[:, part]))
        slopes[:, part] = slope
        spread(silu.astype(BF16), outbox, inbox, kind)

    silu, slope = silu_parts(dot(norm_low, pw[:, :D]))
    slopes[:, :D] = slope
    gate = silu.astype(BF16)
    gate_s[...] = gate
    spread((gg[...] * gate.astype(F32)).astype(BF16), out_c, c_s, 3)
    for kind, inbox in enumerate((q_s, k_s, v_s)):
        settle(inbox.at[pl.ds(0, 3)], ex_r.at[kind])

    def forward(qb, carry):
        big, half = div(qb, 2), pl.ds(pl.multiple_of(rem(qb, 2) * QT, QT), QT)
        query = q_s[big, half, :]

        def tile(kb, total, diagonal):
            half_score = dot(query, k_s[kb], 1, 1) * (0.5 * SCALE)
            t = jnp.tanh(half_score)
            turned = half_score * t
            weights = half_score + turned
            slope = (1.0 + t) * ((1.0 + half_score) - turned) * (0.5 * SCALE)
            if diagonal:
                allowed = (iota((QT, TOK), 1) - iota((QT, TOK), 0)) <= (qb * QT - kb * TOK)
                weights = jnp.where(allowed, weights, 0.0)
                slope = jnp.where(allowed, slope, 0.0)
            weights = weights.astype(BF16)
            w_t[tile_of(big, kb), half, :] = weights
            d_t[tile_of(big, kb), half, :] = slope
            return total + dot(weights, v_s[kb])

        total = lax.fori_loop(0, big, lambda kb, total: tile(kb, total, False), jnp.zeros((QT, HD), F32))
        att[big, half, :] = tile(big, total, True)
        return carry

    lax.fori_loop(0, SEQ // QT, forward, 0)

    settle(c_s.at[pl.ds(0, 3)], ex_r.at[3])
    for b in range(NC):
        total = att[b]
        cot = c_s[b].astype(F32)
        mean = jnp.mean(total, -1, keepdims=True)
        off = total - mean
        spread_sum = jnp.sum(off * off, -1, keepdims=True)
        c_sum = jnp.sum(cot, -1, keepdims=True)
        c_off = jnp.sum(cot * off, -1, keepdims=True)
        lane = iota((TOK, HD), 1)
        table4 = jnp.where(lane == 0, mean, jnp.where(lane == 1, spread_sum, jnp.where(lane == 2, c_sum, c_off)))
        stats[block, :, b * TOK:(b + 1) * TOK] = table4.T[:8]
    for k in range(1, NC):
        remote(stats.at[block], stats.at[block], st_s, st_r, peer(each_peer(k))).start()
    for b in range(NC):
        q_t[b] = q_s[b].astype(F32).T.astype(BF16)
    settle(stats.at[pl.ds(0, 3)], st_r)

    means = [stats[h, 0:1, :] for h in range(NC)]
    mean = (means[0] + means[1] + means[2] + means[3]) * (1.0 / NC)
    spread_sum = 0.0
    c_sum = 0.0
    c_off = 0.0
    for h in range(NC):
        gap = means[h] - mean
        spread_sum = spread_sum + stats[h, 1:2, :] + HD * gap * gap
        c_sum = c_sum + stats[h, 2:3, :]
        c_off = c_off + stats[h, 3:4, :] + stats[h, 2:3, :] * gap
    r_a = lax.rsqrt(spread_sum * (1.0 / D) + EPSILON)
    c_mean = c_sum * (1.0 / D)
    c_norm = r_a * c_off * (1.0 / D)
    sub = iota((8, SEQ), 0)
    rows8 = jnp.where(sub == 0, mean, jnp.where(sub == 1, r_a, jnp.where(sub == 2, c_mean, c_norm)))

    for b in range(NC):
        wide = jnp.concatenate([rows8[:, b * TOK:(b + 1) * TOK]] * 16, axis=0).T
        a_norm = (att[b] - wide[:, 0:1]) * wide[:, 1:2]
        out_an[b] = a_norm.astype(BF16)
        grad = wide[:, 1:2] * (c_s[b].astype(F32) - wide[:, 2:3] - a_norm * wide[:, 3:4])
        d_att[b] = grad.astype(BF16)
        d_att_t[b] = grad.T.astype(BF16)
    for k in range(1, NC):
        j = each_peer(k)
        remote(out_an.at[j], an_s.at[:, pl.ds(head, HD)], ex_s.at[4], ex_r.at[4], peer(j)).start()
    an_s[:, pl.ds(head, HD)] = out_an[block]

    dq_acc[...] = jnp.zeros((NC, TOK, HD), F32)

    def backward(step, carry):
        kb = rem(block + 1 + step, NC)
        d_kv[...] = jnp.zeros((2, HD, TOK), F32)

        def tile(qb, inner):
            slope = dot(d_att[qb], v_s[kb], 1, 1)
            ds = (slope * d_t[tile_of(qb, kb)]).astype(BF16)
            dq_acc[qb] += dot(ds, k_s[kb])
            d_kv[0] += dot(q_t[qb], ds)
            d_kv[1] += dot(d_att_t[qb], w_t[tile_of(qb, kb)])
            return inner

        lax.fori_loop(kb, NC, tile, 0)
        out_dk[kb] = d_kv[0].T.astype(BF16)
        out_dv[kb] = d_kv[1].T.astype(BF16)

        @pl.when(kb != block)
        def _():
            remote(out_dk.at[kb], dqkv.at[:, pl.ds(D + head, HD)], ex_s.at[5], ex_r.at[5], peer(kb)).start()
            remote(out_dv.at[kb], dqkv.at[:, pl.ds(2 * D + head, HD)], ex_s.at[6], ex_r.at[6], peer(kb)).start()

        return carry

    lax.fori_loop(0, 2, backward, 0)

    settle(an_s.at[:, pl.ds(0, 3 * HD)], ex_r.at[4])
    a_norm = an_s[...].astype(F32)
    gated = (a_norm * gate_s[...].astype(F32)).astype(BF16)
    mix[...] = (emb[...].astype(F32) + dot(gated, ow[...])).astype(BF16)

    @pl.when(away)
    def _():
        remote(mix, mixed, mx_s, mx_r, place(held)).start()

    @pl.when(jnp.logical_not(away))
    def _():
        mixed[...] = mix[...]

    e_acc[...] = dot((gg[...] * a_norm * slopes[:, :D]).astype(BF16), pw[:, :D], 1, 1)

    lax.fori_loop(2, NC, backward, 0)
    for b in range(NC):
        out_dq[b] = dq_acc[b].astype(BF16)
    for k in range(1, NC):
        j = each_peer(k)
        remote(out_dq.at[j], dqkv.at[:, pl.ds(head, HD)], ex_s.at[7], ex_r.at[7], peer(j)).start()
    dqkv[:, pl.ds(head, HD)] = out_dq[block]
    dqkv[:, pl.ds(D + head, HD)] = out_dk[block]
    dqkv[:, pl.ds(2 * D + head, HD)] = out_dv[block]

    incoming = e_acc[...]
    for kind, part in ((5, 1), (6, 2), (7, 0)):
        settle(an_s.at[:, pl.ds(0, 3 * HD)], ex_r.at[kind])
        grad = dqkv[:, part * D:(part + 1) * D].astype(F32) * slopes[:, (part + 1) * D:(part + 2) * D]
        incoming = incoming + dot(grad.astype(BF16), pw[:, (part + 1) * D:(part + 2) * D], 1, 1)
    norm = normed[...]
    embed_grad = r_x[...] * (
        incoming
        - jnp.mean(incoming, -1, keepdims=True)
        - norm * jnp.mean(incoming * norm, -1, keepdims=True)
    ) + og[...].astype(F32)
    embed_grad = embed_grad.astype(BF16)

    for step in range(ND // GROUP):
        group = rem(step + div(me, GROUP), ND // GROUP)
        first = pl.multiple_of(group * GROUP, GROUP)
        slots = iota((GROUP * CAP, TOK), 0) + group * (GROUP * CAP)
        sorted_rows = dot(one_hot(slots == slot_line.astype(jnp.int32)), embed_grad)
        halves = [sorted_rows[:, :256].reshape(GROUP, CAP, 256), sorted_rows[:, 256:].reshape(GROUP, CAP, 256)]
        out2[pl.ds(first, GROUP)] = jnp.concatenate(halves, axis=1).astype(BF16)

        def send(k):
            target = first + rem(k + me, GROUP)

            @pl.when(target != me)
            def _():
                remote(out2.at[target], recv2.at[held], b_s, b_r, place(target)).start()

            @pl.when(target == me)
            def _():
                recv2[held] = out2[target]

        members(send)

    settle(vall.at[pl.ds(0, ND - 1)], ids_s)
    settle(out1.at[pl.ds(0, ND - 1)], a_s)
    settle(stats.at[pl.ds(0, 3)], st_s)
    for kind in range(8):
        settle(out_q.at[pl.ds(0, 3)], ex_s.at[kind])

    @pl.when(relay != me)
    def _():
        settle(og_in, og_s.at[0])

    @pl.when(beyond != me)
    def _():
        settle(og_mid, og_s.at[1])

    @pl.when(away)
    def _():
        settle(mix, mx_s)
        settle(mixed, mx_r)

    settle(out2.at[pl.ds(0, ND - 1)], b_s)
    settle(recv2.at[pl.ds(0, ND - 1)], b_r)


def scatter_kernel(wrow, recv2, mix, out, mixed, rows):
    step = pl.program_id(0)

    @pl.when(step == 0)
    def _():
        for g in range(ND // GROUP):
            got = recv2[g * GROUP:(g + 1) * GROUP].astype(F32)
            rows[g * GROUP * CAP:(g + 1) * GROUP * CAP] = jnp.concatenate(
                [got[:, :CAP].reshape(GROUP * CAP, 256), got[:, CAP:].reshape(GROUP * CAP, 256)], axis=1
            ).astype(BF16)

    mixed[...] = mix[...]
    size = out.shape[0]
    wanted = wrow[...].astype(jnp.int32) - step * size
    for part in range(size // 256):
        at = slice(part * 256, (part + 1) * 256)
        out[at, :] = dot(one_hot(iota((256, SLOTS), 0) + part * 256 == wanted), rows[...])


def shards(owner, row, lengths, table, proj_weight, out_weight, out_grad):
    vmem = pl.BlockSpec(memory_space=pltpu.VMEM)
    hbm = pl.BlockSpec(memory_space=pltpu.HBM)
    V = pltpu.VMEM
    DMA = pltpu.SemaphoreType.DMA
    mixed, recv2, wrow = pl.pallas_call(
        layer,
        out_shape=(
            jax.ShapeDtypeStruct((TOK, D), BF16),
            jax.ShapeDtypeStruct((ND, 2 * CAP, 256), BF16),
            jax.ShapeDtypeStruct((1, SLOTS), F32),
        ),
        in_specs=[vmem, vmem, pl.BlockSpec(memory_space=pltpu.SMEM), hbm, hbm, hbm, hbm],
        out_specs=(vmem, vmem, vmem),
        scratch_shapes=[
            V((ROWS, D), BF16), V((D, 4 * D), BF16), V((D, D), BF16), V((TOK, D), BF16), V((TOK, D), BF16), V((TOK, D), BF16),
            V((1, 1, TOK), jnp.int32), V((ND, 1, TOK), jnp.int32),
            V((ND, 2 * CAP, 256), BF16), V((ND, 2 * CAP, 256), BF16), V((TOK, D), BF16),
            V((TOK, D), F32), V((TOK, 1), F32), V((TOK, 4 * D), F32), V((TOK, D), BF16), V((TOK, D), F32),
        ] + [V((NC, TOK, HD), BF16)] * 12 + [
            V((TOK, D), BF16), V((TOK, 3 * D), BF16),
            V((NC, TOK, HD), F32), V((10, TOK, TOK), BF16), V((10, TOK, TOK), F32),
            V((NC, TOK, HD), BF16), V((NC, HD, TOK), BF16), V((NC, HD, TOK), BF16),
            V((NC, TOK, HD), F32), V((2, HD, TOK), F32), V((TOK, D), F32), V((TOK, D), BF16), V((NC, 8, SEQ), F32),
            V((ND, 2 * CAP, 256), BF16),
            DMA((4,)), DMA, DMA, DMA((2,)), DMA((2,)), DMA, DMA, DMA, DMA, DMA((8,)), DMA((8,)), DMA, DMA, DMA, DMA,
        ],
        compiler_params=pltpu.CompilerParams(
            collective_id=0, has_side_effects=True, vmem_limit_bytes=52 * 1024 * 1024
        ),
    )(
        owner.reshape(1, TOK), row.reshape(1, TOK), lengths, table, proj_weight, out_weight,
        out_grad.reshape(TOK, D),
    )
    steps = 4
    table_grad, mixed = pl.pallas_call(
        scatter_kernel,
        grid=(steps,),
        out_shape=(jax.ShapeDtypeStruct((ROWS, D), F32), jax.ShapeDtypeStruct((TOK, D), BF16)),
        in_specs=[vmem, vmem, pl.BlockSpec((TOK // steps, D), lambda i: (i, 0))],
        out_specs=(
            pl.BlockSpec((ROWS // steps, D), lambda i: (i, 0)),
            pl.BlockSpec((TOK // steps, D), lambda i: (i, 0)),
        ),
        scratch_shapes=[V((SLOTS, D), BF16)],
        compiler_params=pltpu.CompilerParams(vmem_limit_bytes=32 * 1024 * 1024),
    )(wrow, recv2, mixed)
    return (mixed.reshape(1, TOK, D), table_grad)


def solution(mesh):
    placed = (
        P("user", "ctx", None),
        P("user", "ctx"),
        P("user"),
        P(("user", "ctx"), None),
        P(),
        P(),
        P("user", "ctx", None),
    )
    return jax.shard_map(
        shards,
        mesh=mesh,
        in_specs=placed,
        out_specs=(P("user", "ctx", None), P(("user", "ctx"), None)),
        check_vma=False,
    )
```

time: 146 us -> 123 us (0.84)
  Pallas kernels: 139 us -> 117 us
    pallas_call x1, Pallas kernels: 134 us -> 113 us  [shards(): pl.pallas_call(layer, out_shape=(jax.ShapeDtypeStruct((TOK, D), BF16), ja...]
    unnamed x11 -> x10, local copies, waits for them, and re-layouts: 5.45 us -> 4.66 us
where the time goes in v1:
time: 123 us
  Pallas kernels  117 us (95%)
  local copies, waits for them, and re-layouts  4.66 us (4%)
  between operations  1.31 us (1%)
    pallas_call x1, Pallas kernels, shards(): pl.pallas_call(layer, out_shape=(jax.ShapeDtypeStruct((TOK, D), BF16), ja...  113 us
    unnamed x10, local copies, waits for them, and re-layouts  4.66 us
    pallas_call x1, Pallas kernels, shards(): pl.pallas_call(scatter_kernel, grid=(steps,), out_shape=(jax.ShapeDtypeSt...  4.15 us

profile of v1, /device:TPU:1, one launch (start us, length us, event | category | flops | bytes accessed | tf_op | source)
XLA Modules:
  0.0 122.9 jit_solution(7218328221152532006)
XLA Ops:
  1.3 0.0 copy-start.1
  1.3 1.0 copy-done.1
  2.3 0.0 copy-start.2
  2.3 1.0 copy-done.2
  3.4 0.0 copy-start.3
  3.4 0.7 copy-done.3
  4.0 0.0 copy-start.4
  4.0 0.7 copy-done.4
  4.7 112.8 %shard_map.86 = (bf16[512,512]{1,0:T(8,128)(2,1)S(1)}, bf16[128,16,256]{2,1,0:T(8,128)(2,1)}, f32[1,1024]{1,0:T(1,128)S(1)}) custom-call(s32[1,512]{1,0:T(1,128)S(1)} %bitcast.4, s32[1,512]{1,0:T(1,128)S(1)} %copy-done.4, s32[1]{0:T(128)S(6)} %copy.9.length, bf16[2048,512]{1,0:T(8,128)(2,1)} %table_h.1, bf16[512,2048]{1,0:T(8,128)(2,1)} %pw_h.1, ...), custom_call_target="tpu_custom_call" | custom-call | tf_op jit(solution)/shard_map/pallas_call | solution.py:499
  117.6 0.0 copy-start
  117.6 1.2 copy-done
  118.8 4.2 %shard_map.87 = (f32[2048,512]{1,0:T(8,128)}, bf16[512,512]{1,0:T(8,128)(2,1)}) custom-call(f32[1,1024]{1,0:T(1,128)S(1)} %get-tuple-element.7.wrow, bf16[128,16,256]{2,1,0:T(8,128)(2,1)S(1)} %copy-done, bf16[512,512]{1,0:T(8,128)(2,1)S(1)} %get-tuple-element.9.mix), custom_call_target="tpu_custom_call" | custom-call | tf_op jit(solution)/shard_map/pallas_call | solution.py:529
Async XLA Ops:
  1.3 1.0 copy-start.1
  2.3 1.0 copy-start.2
  3.4 0.7 copy-start.3
  4.0 0.7 copy-start.4
  117.6 1.2 copy-start

commit v2 on v1

v2 whole, which is shorter than its diff:
```python
import jax
import jax.numpy as jnp
from jax import lax
from jax.experimental import pallas as pl
from jax.experimental.pallas import tpu as pltpu
from jax.sharding import PartitionSpec as P

MESH = pl.DeviceIdType.MESH
F32 = jnp.float32
BF16 = jnp.bfloat16
NC = 4
ND = 128
TOK = 512
SEQ = 2048
D = 512
HD = 128
CAP = 8
ROWS = 2048
SLOTS = ND * CAP
GROUP = 32
EPSILON = 1e-05
SCALE = HD ** (-0.5)
QT = 256


def div(a, b):
    return lax.div(a, jnp.int32(b))


def rem(a, b):
    return lax.rem(a, jnp.int32(b))


SETS = sorted(((dy, dz) for dy in range(4) for dz in range(4)), key=lambda d: -((0, 1, 2, 1)[d[0]] + (0, 1, 2, 1)[d[1]]))
HERE = SETS.index((0, 0)) * 8


def opposite_set(k):
    return SETS.index(((4 - SETS[k][0]) % 4, (4 - SETS[k][1]) % 4))


def opposite_member(k):
    return k // 4 * 4 + (4 - k % 4) % 4


def opposite(k):
    return opposite_set(k // 8) * 8 + opposite_member(k % 8)


def order_of(first):
    far = (0, 1, 2, 1)
    return sorted(
        range(first, first + GROUP),
        key=lambda k: -(far[SETS[k // 8][0]] + far[SETS[k // 8][1]] + far[k % 4]),
    )


def iota(shape, axis):
    return lax.broadcasted_iota(jnp.int32, shape, axis)


def to_column(line):
    n = line.shape[1]
    eye = iota((n, n), 0) == iota((n, n), 1)
    return jnp.sum(jnp.where(eye, line, 0.0), axis=1, keepdims=True)


def to_line(column):
    n = column.shape[0]
    eye = iota((n, n), 0) == iota((n, n), 1)
    return jnp.sum(jnp.where(eye, column, 0.0), axis=0, keepdims=True)


def one_hot(match):
    return jnp.where(match, 1.0, 0.0).astype(BF16)


def dot(a, b, ca=1, cb=0):
    return lax.dot_general(a, b, (((ca,), (cb,)), ((), ())), preferred_element_type=F32)


def remote(src, dst, send, recv, target):
    return pltpu.make_async_remote_copy(
        src_ref=src, dst_ref=dst, send_sem=send, recv_sem=recv, device_id=target, device_id_type=MESH
    )


def tile_of(q, k):
    return div(q * (q + 1), 2) + k


def settle(view, sem):
    pltpu.make_async_copy(view, view, sem).wait()


def silu_parts(values):
    half = values * 0.5
    t = jnp.tanh(half)
    turned = half * t
    return half + turned, (0.5 + 0.5 * t) * (1.0 + (half - turned))


def layer(
    owner, row, length, table_h, pw_h, ow_h, og_h,
    mixed, recv2, wrow,
    table, pw, ow, og, og_in, og_mid, v_out, v_held, ask_out, ask_mid, ask_in, out1, recv1, emb, normed, r_x, slopes, gate_s, gg,
    out_q, out_k, out_v, out_off, out_da, out_dk, out_dv, out_dq, q_s, k_s, v_s, da_s, off_s, dqkv, out_m, m_s,
    an_s, att, w_t, d_t, da_t, q_t, dq_acc, d_kv, e_acc, mix, out2,
    load, ids_s, ids_r, og_s, og_r, a_s, a_r, ex_s, ex_r, mx_s, mx_r, b_s, b_r,
):
    user, ctx = lax.axis_index("user"), lax.axis_index("ctx")
    core, z_at, y_at = rem(user, 2), rem(div(user, 2), 4), div(user, 8)

    def device(x, y, z=z_at, c=core):
        return ((y * 4 + z) * 2 + c, x)

    xs = [rem(ctx + d, 4) for d in range(4)]
    ys = [rem(y_at + d, 4) for d in range(4)]
    zs = [rem(z_at + d, 4) for d in range(4)]
    cores = [core, 1 - core]

    def place(k):
        dy, dz = SETS[k // 8]
        return device(xs[k % 4], ys[dy], zs[dz], cores[k % 8 // 4])

    work_x, work_y = ctx + core * (y_at - ctx), y_at + core * (rem(ctx + y_at, 4) - y_at)
    back = rem(y_at + 4 - ctx, 4)
    held_x, held_y = ctx + core * (back - ctx), y_at + core * (ctx - y_at)
    block = held_x
    away = jnp.logical_or(work_x != ctx, work_y != y_at)
    relay_away, beyond_away = work_y != y_at, held_x != ctx

    def peer(j):
        other = (rem(j + ctx, 4) * 4 + z_at) * 2 + 1
        return (user + core * (other - user), j + core * (ctx - j))

    def each_peer(k):
        return rem(block + k, NC)

    barrier = pltpu.get_barrier_semaphore()

    for k in range(ND):
        if k != HERE:
            pl.semaphore_signal(barrier, inc=1, device_id=place(k), device_id_type=MESH)

    head = pl.multiple_of(block * HD, HD)
    loads = [
        pltpu.make_async_copy(og_h, og_in, load.at[0]),
        pltpu.make_async_copy(table_h, table, load.at[1]),
        pltpu.make_async_copy(ow_h, ow, load.at[2]),
        pltpu.make_async_copy(pw_h, pw, load.at[3]),
    ]
    for copy in loads:
        copy.start()

    places = ctx * TOK + iota((1, TOK), 1)
    valid = places < length[0]
    who = owner[...]
    far_x = jnp.bitwise_and(who + (4 - work_x), 3)
    far_core = jnp.bitwise_and(lax.shift_right_logical(who, 2) + core, 1)
    far_z = jnp.bitwise_and(lax.shift_right_logical(who, 3) + (4 - z_at), 3)
    far_y = jnp.bitwise_and(lax.shift_right_logical(who, 5) + (4 - work_y), 3)
    far_set = jnp.zeros((1, TOK), jnp.int32)
    for number, (dy, dz) in enumerate(SETS):
        far_set = jnp.where(far_y * 4 + far_z == dy * 4 + dz, number, far_set)
    own = jnp.where(valid, far_set * 8 + far_core * 4 + far_x, -1)
    match = iota((ND, TOK), 0) == own
    before = one_hot(iota((TOK, TOK), 0) < iota((TOK, TOK), 1))
    rank = dot(one_hot(match), before)
    slot = jnp.sum(jnp.where(match, rank, 0.0), axis=0, keepdims=True).astype(jnp.int32)
    slot_own = jnp.where(valid, own * CAP + slot, -1)
    v_out[0] = slot_own

    lane_own = jnp.where(valid, lax.shift_right_arithmetic(own, 3) * CAP + slot, -1)
    lanes_hot = one_hot(iota((TOK, ND), 1) == to_column(lane_own.astype(F32)).astype(jnp.int32))
    sub16 = iota((16, TOK), 0)
    digits = jnp.where(sub16 < 8, lax.shift_right_arithmetic(row[...] + 1, 6), jnp.bitwise_and(row[...] + 1, 63))
    digits = jnp.where(jnp.bitwise_and(sub16, 7) == far_core * 4 + far_x, digits, 0).astype(F32).astype(BF16)
    lines = dot(digits, lanes_hot)
    lines = lines[:8] * 64.0 + lines[8:]
    for member in range(8):
        ask_out[member] = lines[member:member + 1]

    pl.semaphore_wait(barrier, ND - 1)

    for member in range(8):
        line_x, line_core = rem(work_x + member % 4, 4), rem(core + member // 4, 2)
        here = jnp.logical_and(jnp.logical_and(line_x == ctx, line_core == core), work_y == y_at)

        @pl.when(jnp.logical_not(here))
        def _():
            target = device(line_x, work_y, z_at, line_core)
            line = ask_mid.at[opposite_member(member)]
            remote(ask_out.at[member], line, ids_s.at[0], ids_r.at[0], target).start()

        @pl.when(here)
        def _():
            ask_mid[opposite_member(member)] = ask_out[member]

    @pl.when(away)
    def _():
        remote(v_out, v_held, ids_s.at[2], ids_r.at[2], device(work_x, work_y)).start()

    @pl.when(jnp.logical_not(away))
    def _():
        v_held[0] = slot_own

    loads[0].wait()

    @pl.when(relay_away)
    def _():
        remote(og_in, og_mid, og_s.at[0], og_r.at[0], device(ctx, work_y)).start()

    @pl.when(jnp.logical_not(relay_away))
    def _():
        og_mid[...] = og_in[...]

    @pl.when(relay_away)
    def _():
        settle(ask_mid, ids_r.at[0])

    @pl.when(jnp.logical_not(relay_away))
    def _():
        settle(ask_mid.at[pl.ds(0, 7)], ids_r.at[0])

    for number in range(16):
        if number * 8 != HERE:
            lines = ask_in.at[pl.ds(opposite_set(number) * 8, 8)]
            remote(ask_mid, lines, ids_s.at[1], ids_r.at[1], place(number * 8)).start()
    ask_in[HERE:HERE + 8] = ask_mid[...]
    settle(ask_in.at[pl.ds(0, 120)], ids_r.at[1])
    loads[1].wait()

    for first in range(0, ND, GROUP):
        wanted = []
        for number in range(first // 8, (first + GROUP) // 8):
            mine = iota((1, CAP, ND), 2) == iota((1, CAP, ND), 1) + opposite_set(number) * CAP
            lines = jnp.where(mine, ask_in[number * 8:number * 8 + 8], 0.0)
            wanted.append(jnp.sum(lines, axis=2, keepdims=True).reshape(8 * CAP, 1))
        wanted = jnp.concatenate(wanted, axis=0) - 1.0
        wrow[:, first * CAP:(first + GROUP) * CAP] = to_line(wanted)
        found = dot(one_hot(iota((GROUP * CAP, ROWS), 1) == wanted.astype(jnp.int32)), table[...])
        halves = [found[:, :256].reshape(GROUP, CAP, 256), found[:, 256:].reshape(GROUP, CAP, 256)]
        out1[first:first + GROUP] = jnp.concatenate(halves, axis=1).astype(BF16)
        for k in order_of(first):
            if k != HERE:
                remote(out1.at[k], recv1.at[opposite(k)], a_s, a_r, place(k)).start()
    recv1[HERE] = out1[HERE]

    @pl.when(away)
    def _():
        settle(v_held, ids_r.at[2])

    slot_line = v_held[0].astype(F32)
    slot_col = to_column(slot_line)
    loads[2].wait()
    loads[3].wait()

    settle(recv1.at[pl.ds(0, ND - 1)], a_r)
    embed = jnp.zeros((TOK, D), F32)
    for g in range(ND // GROUP):
        got = recv1[g * GROUP:(g + 1) * GROUP].astype(F32)
        rows = jnp.concatenate(
            [got[:, :CAP].reshape(GROUP * CAP, 256), got[:, CAP:].reshape(GROUP * CAP, 256)], axis=1
        ).astype(BF16)
        lanes = iota((TOK, GROUP * CAP), 1) + g * GROUP * CAP
        embed = embed + dot(one_hot(lanes == slot_col.astype(jnp.int32)), rows)
    emb[...] = embed.astype(BF16)
    center = jnp.mean(embed, -1, keepdims=True)
    deviation = embed - center
    inverse = lax.rsqrt(jnp.mean(deviation * deviation, -1, keepdims=True) + EPSILON)
    norm = deviation * inverse
    normed[...] = norm
    r_x[...] = inverse
    norm_low = norm.astype(BF16)

    for kind, (outbox, inbox) in enumerate(((out_q, q_s), (out_k, k_s), (out_v, v_s))):
        part = slice((kind + 1) * D, (kind + 2) * D)
        silu, slope = silu_parts(dot(norm_low, pw[:, part]))
        slopes[:, part] = slope
        low = silu.astype(BF16)
        for j in range(NC):
            outbox[j] = low[:, j * HD:(j + 1) * HD]
        inbox[block] = outbox[block]
    for k in (1, 3, 2):
        j = each_peer(k)
        for outbox, inbox in ((out_q, q_s), (out_k, k_s), (out_v, v_s)):
            remote(outbox.at[j], inbox.at[block], ex_s.at[k - 1], ex_r.at[k - 1], peer(j)).start()

    silu, slope = silu_parts(dot(norm_low, pw[:, :D]))
    slopes[:, :D] = slope
    gate_s[...] = silu.astype(BF16)

    def tile(qb, kb, diagonal):
        for part in range(TOK // QT):
            half = slice(part * QT, (part + 1) * QT)
            half_score = dot(q_s[qb, half, :], k_s[kb], 1, 1) * (0.5 * SCALE)
            t = jnp.tanh(half_score)
            turned = half_score * t
            weights = half_score + turned
            slope = (1.0 + t) * ((1.0 + half_score) - turned) * (0.5 * SCALE)
            if diagonal:
                allowed = (iota((QT, TOK), 1) - iota((QT, TOK), 0)) <= part * QT
                weights = jnp.where(allowed, weights, 0.0)
                slope = jnp.where(allowed, slope, 0.0)
            weights = weights.astype(BF16)
            w_t[tile_of(qb, kb), half, :] = weights
            d_t[tile_of(qb, kb), half, :] = slope.astype(BF16)
            if diagonal:
                att[qb, half, :] = dot(weights, v_s[kb])
            else:
                att[qb, half, :] += dot(weights, v_s[kb])

    def finish(qb):
        for part in range(TOK // QT):
            half = slice(part * QT, (part + 1) * QT)
            total = att[qb, half, :]
            mean = jnp.mean(total, -1, keepdims=True)
            out_off[qb, half, :] = (total - mean).astype(BF16)
            out_m[qb, :, half] = to_line(mean)

        @pl.when(qb != block)
        def _():
            remote(out_off.at[qb], off_s.at[:, pl.ds(head, HD)], ex_s.at[3], ex_r.at[3], peer(qb)).start()
            remote(out_m.at[qb], m_s.at[block], ex_s.at[4], ex_r.at[4], peer(qb)).start()

    after, across, ahead = rem(block + 1, NC), rem(block + 2, NC), rem(block + 3, NC)
    tile(block, block, True)
    settle(q_s.at[pl.ds(0, 3)], ex_r.at[0])
    settle(q_s.at[pl.ds(0, 3)], ex_r.at[2])

    def diagonals(step, carry):
        b = rem(block + 1 + 2 * step, NC)
        tile(b, b, True)
        return carry

    def near_pairs(step, carry):
        one = jnp.where(step == 2, after, block)
        two = jnp.where(step == 0, after, ahead)
        tile(jnp.maximum(one, two), jnp.minimum(one, two), False)
        return carry

    lax.fori_loop(0, 2, diagonals, 0)
    lax.fori_loop(0, 3, near_pairs, 0)
    settle(q_s.at[pl.ds(0, 3)], ex_r.at[1])

    @pl.when(relay_away)
    def _():
        settle(og_mid, og_r.at[0])

    @pl.when(beyond_away)
    def _():
        remote(og_mid, og, og_s.at[1], og_r.at[1], device(held_x, y_at)).start()

    def near_rows(step, carry):
        qb = rem(block + 1 + 2 * step, NC)

        @pl.when(qb > across)
        def _():
            tile(qb, across, False)

        finish(qb)
        return carry

    lax.fori_loop(0, 2, near_rows, 0)
    tile(across, across, True)

    def far_row(kb, carry):
        tile(across, kb, False)
        return carry

    lax.fori_loop(0, across, far_row, 0)
    finish(across)

    @pl.when(block > across)
    def _():
        tile(block, across, False)

    finish(block)
    off_s[:, pl.ds(head, HD)] = out_off[block]
    m_s[block] = out_m[block]

    @pl.when(beyond_away)
    def _():
        settle(og, og_r.at[1])

    @pl.when(jnp.logical_not(beyond_away))
    def _():
        og[...] = og_mid[...]

    masked = jnp.where(slot_col >= 0.0, og[...], jnp.zeros((TOK, D), BF16))
    og[...] = masked
    gg[...] = dot(masked, ow[...], 1, 1)

    settle(off_s.at[:, pl.ds(0, 3 * HD)], ex_r.at[3])
    settle(m_s.at[pl.ds(0, 3)], ex_r.at[4])
    m_all = (m_s[0] + m_s[1] + m_s[2] + m_s[3]) * (1.0 / NC)
    for part in range(TOK // QT):
        half = slice(part * QT, (part + 1) * QT)
        off = off_s[half, :].astype(F32)
        gaps = [to_column((m_s[h] - m_all)[:, half]) for h in range(NC)]
        off = jnp.concatenate([off[:, h * HD:(h + 1) * HD] + gaps[h] for h in range(NC)], axis=1)
        deviation = off - jnp.mean(off, -1, keepdims=True)
        r_a = lax.rsqrt(jnp.mean(deviation * deviation, -1, keepdims=True) + EPSILON)
        a_norm = deviation * r_a
        an_s[half, :] = a_norm
        cot = gg[half, :] * gate_s[half, :].astype(F32)
        grad = r_a * (
            cot - jnp.mean(cot, -1, keepdims=True) - a_norm * jnp.mean(cot * a_norm, -1, keepdims=True)
        )
        grad = grad.astype(BF16)
        for j in range(NC):
            out_da[j, half, :] = grad[:, j * HD:(j + 1) * HD]
        for k in range(1, NC):
            j = each_peer(k)
            rows = pl.ds(part * QT, QT)
            remote(out_da.at[j, rows], da_s.at[block, rows], ex_s.at[5], ex_r.at[5], peer(j)).start()
    da_s[block] = out_da[block]

    a_norm = an_s[...]
    gated = (a_norm * gate_s[...].astype(F32)).astype(BF16)
    mix[...] = (emb[...].astype(F32) + dot(gated, ow[...])).astype(BF16)

    @pl.when(away)
    def _():
        remote(mix, mixed, mx_s, mx_r, device(held_x, held_y)).start()

    @pl.when(jnp.logical_not(away))
    def _():
        mixed[...] = mix[...]

    e_acc[...] = dot((gg[...] * a_norm * slopes[:, :D]).astype(BF16), pw[:, :D], 1, 1)
    for b in range(NC):
        q_t[b] = q_s[b].astype(F32).T.astype(BF16)

    def by_row(qb):
        grad = da_s[qb]
        dq_acc[...] = jnp.zeros((TOK, HD), F32)

        def tile(kb, carry):
            slope = dot(grad, v_s[kb], 1, 1)
            ds = (slope * d_t[tile_of(qb, kb)].astype(F32)).astype(BF16)
            d_t[tile_of(qb, kb)] = ds
            dq_acc[...] += dot(ds, k_s[kb])
            return carry

        lax.fori_loop(0, qb + 1, tile, 0)
        out_dq[qb] = dq_acc[...].astype(BF16)
        da_t[qb] = grad.astype(F32).T.astype(BF16)

    by_row(block)
    settle(da_s.at[pl.ds(0, 3)], ex_r.at[5])

    def other_row(k, carry):
        qb = each_peer(k)
        by_row(qb)
        remote(out_dq.at[qb], dqkv.at[:, pl.ds(head, HD)], ex_s.at[6], ex_r.at[6], peer(qb)).start()
        return carry

    lax.fori_loop(1, NC, other_row, 0)

    def by_column(step, carry):
        kb = rem(block + 1 + step, NC)
        d_kv[...] = jnp.zeros((2, HD, TOK), F32)

        def tile(qb, inner):
            d_kv[0] += dot(q_t[qb], d_t[tile_of(qb, kb)])
            d_kv[1] += dot(da_t[qb], w_t[tile_of(qb, kb)])
            return inner

        lax.fori_loop(kb, NC, tile, 0)
        out_dk[kb] = d_kv[0].T.astype(BF16)
        out_dv[kb] = d_kv[1].T.astype(BF16)

        @pl.when(kb != block)
        def _():
            remote(out_dk.at[kb], dqkv.at[:, pl.ds(D + head, HD)], ex_s.at[7], ex_r.at[7], peer(kb)).start()
            remote(out_dv.at[kb], dqkv.at[:, pl.ds(2 * D + head, HD)], ex_s.at[8], ex_r.at[8], peer(kb)).start()

        return carry

    lax.fori_loop(0, NC, by_column, 0)
    dqkv[:, pl.ds(head, HD)] = out_dq[block]
    dqkv[:, pl.ds(D + head, HD)] = out_dk[block]
    dqkv[:, pl.ds(2 * D + head, HD)] = out_dv[block]

    incoming = e_acc[...]
    for kind, part in ((6, 0), (7, 1), (8, 2)):
        settle(off_s.at[:, pl.ds(0, 3 * HD)], ex_r.at[kind])
        grad = dqkv[:, part * D:(part + 1) * D].astype(F32) * slopes[:, (part + 1) * D:(part + 2) * D]
        incoming = incoming + dot(grad.astype(BF16), pw[:, (part + 1) * D:(part + 2) * D], 1, 1)
    norm = normed[...]
    embed_grad = r_x[...] * (
        incoming
        - jnp.mean(incoming, -1, keepdims=True)
        - norm * jnp.mean(incoming * norm, -1, keepdims=True)
    ) + og[...].astype(F32)
    embed_grad = embed_grad.astype(BF16)

    for first in range(0, ND, GROUP):
        slots = iota((GROUP * CAP, TOK), 0) + first * CAP
        sorted_rows = dot(one_hot(slots == slot_line.astype(jnp.int32)), embed_grad)
        halves = [sorted_rows[:, :256].reshape(GROUP, CAP, 256), sorted_rows[:, 256:].reshape(GROUP, CAP, 256)]
        out2[first:first + GROUP] = jnp.concatenate(halves, axis=1).astype(BF16)
        for k in order_of(first):
            if k != HERE:
                remote(out2.at[k], recv2.at[opposite(k)], b_s, b_r, place(k)).start()
    recv2[HERE] = out2[HERE]

    @pl.when(relay_away)
    def _():
        settle(ask_mid, ids_s.at[0])

    @pl.when(jnp.logical_not(relay_away))
    def _():
        settle(ask_mid.at[pl.ds(0, 7)], ids_s.at[0])

    settle(ask_in.at[pl.ds(0, 120)], ids_s.at[1])
    settle(out1.at[pl.ds(0, ND - 1)], a_s)
    for kind in (0, 1, 2, 3, 5, 6, 7, 8):
        settle(out_q.at[pl.ds(0, 3)], ex_s.at[kind])
    settle(out_m.at[pl.ds(0, 3)], ex_s.at[4])

    @pl.when(relay_away)
    def _():
        settle(og_in, og_s.at[0])

    @pl.when(beyond_away)
    def _():
        settle(og_mid, og_s.at[1])

    @pl.when(away)
    def _():
        settle(v_out, ids_s.at[2])
        settle(mix, mx_s)
        settle(mixed, mx_r)

    settle(out2.at[pl.ds(0, ND - 1)], b_s)
    settle(recv2.at[pl.ds(0, ND - 1)], b_r)


def scatter_kernel(wrow, recv2, mix, out, mixed, rows):
    step = pl.program_id(0)

    @pl.when(step == 0)
    def _():
        for g in range(ND // GROUP):
            got = recv2[g * GROUP:(g + 1) * GROUP].astype(F32)
            rows[g * GROUP * CAP:(g + 1) * GROUP * CAP] = jnp.concatenate(
                [got[:, :CAP].reshape(GROUP * CAP, 256), got[:, CAP:].reshape(GROUP * CAP, 256)], axis=1
            ).astype(BF16)

    mixed[...] = mix[...]
    size = out.shape[0]
    wanted = wrow[...].astype(jnp.int32) - step * size
    for part in range(size // 256):
        at = slice(part * 256, (part + 1) * 256)
        out[at, :] = dot(one_hot(iota((256, SLOTS), 0) + part * 256 == wanted), rows[...])


def shards(owner, row, lengths, table, proj_weight, out_weight, out_grad):
    vmem = pl.BlockSpec(memory_space=pltpu.VMEM)
    hbm = pl.BlockSpec(memory_space=pltpu.HBM)
    V = pltpu.VMEM
    DMA = pltpu.SemaphoreType.DMA
    mixed, recv2, wrow = pl.pallas_call(
        layer,
        out_shape=(
            jax.ShapeDtypeStruct((TOK, D), BF16),
            jax.ShapeDtypeStruct((ND, 2 * CAP, 256), BF16),
            jax.ShapeDtypeStruct((1, SLOTS), F32),
        ),
        in_specs=[vmem, vmem, pl.BlockSpec(memory_space=pltpu.SMEM), hbm, hbm, hbm, hbm],
        out_specs=(vmem, vmem, vmem),
        scratch_shapes=[
            V((ROWS, D), BF16), V((D, 4 * D), BF16), V((D, D), BF16), V((TOK, D), BF16), V((TOK, D), BF16), V((TOK, D), BF16),
            V((1, 1, TOK), jnp.int32), V((1, 1, TOK), jnp.int32), V((8, 1, ND), F32), V((8, 1, ND), F32), V((ND, 1, ND), F32),
            V((ND, 2 * CAP, 256), BF16), V((ND, 2 * CAP, 256), BF16), V((TOK, D), BF16),
            V((TOK, D), F32), V((TOK, 1), F32), V((TOK, 4 * D), F32), V((TOK, D), BF16), V((TOK, D), F32),
        ] + [V((NC, TOK, HD), BF16)] * 12 + [
            V((TOK, D), BF16), V((TOK, 3 * D), BF16), V((NC, 1, TOK), F32), V((NC, 1, TOK), F32),
            V((TOK, D), F32), V((NC, TOK, HD), F32), V((10, TOK, TOK), BF16), V((10, TOK, TOK), BF16),
            V((NC, HD, TOK), BF16), V((NC, HD, TOK), BF16),
            V((TOK, HD), F32), V((2, HD, TOK), F32), V((TOK, D), F32), V((TOK, D), BF16),
            V((ND, 2 * CAP, 256), BF16),
            DMA((4,)), DMA((3,)), DMA((3,)), DMA((2,)), DMA((2,)), DMA, DMA, DMA((9,)), DMA((9,)), DMA, DMA, DMA, DMA,
        ],
        compiler_params=pltpu.CompilerParams(
            collective_id=0, has_side_effects=True, vmem_limit_bytes=52 * 1024 * 1024
        ),
    )(
        owner.reshape(1, TOK), row.reshape(1, TOK), lengths, table, proj_weight, out_weight,
        out_grad.reshape(TOK, D),
    )
    steps = 4
    table_grad, mixed = pl.pallas_call(
        scatter_kernel,
        grid=(steps,),
        out_shape=(jax.ShapeDtypeStruct((ROWS, D), F32), jax.ShapeDtypeStruct((TOK, D), BF16)),
        in_specs=[vmem, vmem, pl.BlockSpec((TOK // steps, D), lambda i: (i, 0))],
        out_specs=(
            pl.BlockSpec((ROWS // steps, D), lambda i: (i, 0)),
            pl.BlockSpec((TOK // steps, D), lambda i: (i, 0)),
        ),
        scratch_shapes=[V((SLOTS, D), BF16)],
        compiler_params=pltpu.CompilerParams(vmem_limit_bytes=32 * 1024 * 1024),
    )(wrow, recv2, mixed)
    return (mixed.reshape(1, TOK, D), table_grad)


def solution(mesh):
    placed = (
        P("user", "ctx", None),
        P("user", "ctx"),
        P("user"),
        P(("user", "ctx"), None),
        P(),
        P(),
        P("user", "ctx", None),
    )
    return jax.shard_map(
        shards,
        mesh=mesh,
        in_specs=placed,
        out_specs=(P("user", "ctx", None), P(("user", "ctx"), None)),
        check_vma=False,
    )
```

time: 123 us -> 114 us (0.927)
  Pallas kernels: 117 us -> 107 us
    pallas_call x1, Pallas kernels: 113 us -> 103 us  [shards(): pl.pallas_call(layer, out_shape=(jax.ShapeDtypeStruct((TOK, D), BF16), ja...]
where the time goes in v2:
time: 114 us; the launch traced here: 113 us
  Pallas kernels  107 us (94%)
  local copies, waits for them, and re-layouts  4.66 us (4%)
  between operations  1.31 us (1%)
    pallas_call x1, Pallas kernels, shards(): pl.pallas_call(layer, out_shape=(jax.ShapeDtypeStruct((TOK, D), BF16), ja...  103 us
    unnamed x10, local copies, waits for them, and re-layouts  4.66 us
    pallas_call x1, Pallas kernels, shards(): pl.pallas_call(scatter_kernel, grid=(steps,), out_shape=(jax.ShapeDtypeSt...  4.15 us

profile of v2, /device:TPU:1, one launch (start us, length us, event | category | flops | bytes accessed | tf_op | source)
XLA Modules:
  0.0 112.9 jit_solution(16731618483290331555)
XLA Ops:
  1.3 0.0 copy-start.1
  1.3 1.0 copy-done.1
  2.3 0.0 copy-start.2
  2.3 1.0 copy-done.2
  3.4 0.0 copy-start.3
  3.4 0.7 copy-done.3
  4.0 0.0 copy-start.4
  4.0 0.7 copy-done.4
  4.7 102.8 %shard_map.86 = (bf16[512,512]{1,0:T(8,128)(2,1)S(1)}, bf16[128,16,256]{2,1,0:T(8,128)(2,1)}, f32[1,1024]{1,0:T(1,128)S(1)}) custom-call(s32[1,512]{1,0:T(1,128)S(1)} %bitcast.4, s32[1,512]{1,0:T(1,128)S(1)} %copy-done.4, s32[1]{0:T(128)S(6)} %copy.9.length, bf16[2048,512]{1,0:T(8,128)(2,1)} %table_h.1, bf16[512,2048]{1,0:T(8,128)(2,1)} %pw_h.1, ...), custom_call_target="tpu_custom_call" | custom-call | tf_op jit(solution)/shard_map/pallas_call | solution.py:566
  107.5 0.0 copy-start
  107.5 1.2 %copy-done = bf16[128,16,256]{2,1,0:T(8,128)(2,1)S(1)} copy-done((bf16[128,16,256]{2,1,0:T(8,128)(2,1)S(1)}, bf16[128,16,256]{2,1,0:T(8,128)(2,1)}, u32[]{:S(2)}) %copy-start) | copy-done | bytes 1048600
  108.7 4.1 %shard_map.87 = (f32[2048,512]{1,0:T(8,128)}, bf16[512,512]{1,0:T(8,128)(2,1)}) custom-call(f32[1,1024]{1,0:T(1,128)S(1)} %get-tuple-element.7.wrow, bf16[128,16,256]{2,1,0:T(8,128)(2,1)S(1)} %copy-done, bf16[512,512]{1,0:T(8,128)(2,1)S(1)} %get-tuple-element.9.mix), custom_call_target="tpu_custom_call" | custom-call | tf_op jit(solution)/shard_map/pallas_call | solution.py:596
Async XLA Ops:
  1.3 1.0 copy-start.1
  2.3 1.0 copy-start.2
  3.4 0.7 copy-start.3
  4.0 0.7 copy-start.4
  107.5 1.2 %copy-start = (bf16[128,16,256]{2,1,0:T(8,128)(2,1)S(1)}, bf16[128,16,256]{2,1,0:T(8,128)(2,1)}, u32[]{:S(2)}) copy-start(bf16[128,16,256]{2,1,0:T(8,128)(2,1)} %get-tuple-element.8.recv2) | copy-start | bytes 3145732

commit v3 on v2

--- a/solution.py
+++ b/solution.py
@@ -101,9 +101,9 @@
 
 
 def layer(
-    owner, row, length, table_h, pw_h, ow_h, og_h,
+    owner_h, row_h, length, table_h, pw_h, ow_h, og_h,
     mixed, recv2, wrow,
-    table, pw, ow, og, og_in, og_mid, v_out, v_held, ask_out, ask_mid, ask_in, out1, recv1, emb, normed, r_x, slopes, gate_s, gg,
+    owner, row, table, pw, ow, og, og_in, og_mid, v_out, v_held, ask_out, ask_mid, ask_in, out1, recv1, emb, normed, r_x, slopes, gate_s, gg,
     out_q, out_k, out_v, out_off, out_da, out_dk, out_dv, out_dq, q_s, k_s, v_s, da_s, off_s, dqkv, out_m, m_s,
     an_s, att, w_t, d_t, da_t, q_t, dq_acc, d_kv, e_acc, mix, out2,
     load, ids_s, ids_r, og_s, og_r, a_s, a_r, ex_s, ex_r, mx_s, mx_r, b_s, b_r,
@@ -139,19 +139,24 @@
 
     barrier = pltpu.get_barrier_semaphore()
 
-    for k in range(ND):
-        if k != HERE:
-            pl.semaphore_signal(barrier, inc=1, device_id=place(k), device_id_type=MESH)
-
     head = pl.multiple_of(block * HD, HD)
     loads = [
         pltpu.make_async_copy(og_h, og_in, load.at[0]),
         pltpu.make_async_copy(table_h, table, load.at[1]),
         pltpu.make_async_copy(ow_h, ow, load.at[2]),
         pltpu.make_async_copy(pw_h, pw, load.at[3]),
+        pltpu.make_async_copy(owner_h, owner, load.at[4]),
+        pltpu.make_async_copy(row_h, row, load.at[5]),
     ]
-    for copy in loads:
+    for copy in reversed(loads):
         copy.start()
+
+    for k in range(ND):
+        if k != HERE:
+            pl.semaphore_signal(barrier, inc=1, device_id=place(k), device_id_type=MESH)
+
+    loads[4].wait()
+    loads[5].wait()
 
     places = ctx * TOK + iota((1, TOK), 1)
     valid = places < length[0]
@@ -282,10 +287,13 @@
         for j in range(NC):
             outbox[j] = low[:, j * HD:(j + 1) * HD]
         inbox[block] = outbox[block]
-    for k in (1, 3, 2):
+    def hand_on(k):
         j = each_peer(k)
         for outbox, inbox in ((out_q, q_s), (out_k, k_s), (out_v, v_s)):
             remote(outbox.at[j], inbox.at[block], ex_s.at[k - 1], ex_r.at[k - 1], peer(j)).start()
+
+    hand_on(1)
+    hand_on(3)
 
     silu, slope = silu_parts(dot(norm_low, pw[:, :D]))
     slopes[:, :D] = slope
@@ -326,6 +334,9 @@
 
     after, across, ahead = rem(block + 1, NC), rem(block + 2, NC), rem(block + 3, NC)
     tile(block, block, True)
+    settle(out_q.at[pl.ds(0, 3)], ex_s.at[0])
+    settle(out_q.at[pl.ds(0, 3)], ex_s.at[2])
+    hand_on(2)
     settle(q_s.at[pl.ds(0, 3)], ex_r.at[0])
     settle(q_s.at[pl.ds(0, 3)], ex_r.at[2])
 
@@ -517,7 +528,7 @@
 
     settle(ask_in.at[pl.ds(0, 120)], ids_s.at[1])
     settle(out1.at[pl.ds(0, ND - 1)], a_s)
-    for kind in (0, 1, 2, 3, 5, 6, 7, 8):
+    for kind in (1, 3, 5, 6, 7, 8):
         settle(out_q.at[pl.ds(0, 3)], ex_s.at[kind])
     settle(out_m.at[pl.ds(0, 3)], ex_s.at[4])
 
@@ -539,12 +550,18 @@
     settle(recv2.at[pl.ds(0, ND - 1)], b_r)
 
 
-def scatter_kernel(wrow, recv2, mix, out, mixed, rows):
+def scatter_kernel(wrow, recv2_h, mix, out, mixed, rows, recv2, load):
     step = pl.program_id(0)
 
     @pl.when(step == 0)
     def _():
+        copies = []
         for g in range(ND // GROUP):
+            part = pl.ds(g * GROUP, GROUP)
+            copies.append(pltpu.make_async_copy(recv2_h.at[part], recv2.at[part], load.at[g]))
+            copies[g].start()
+        for g in range(ND // GROUP):
+            copies[g].wait()
             got = recv2[g * GROUP:(g + 1) * GROUP].astype(F32)
             rows[g * GROUP * CAP:(g + 1) * GROUP * CAP] = jnp.concatenate(
                 [got[:, :CAP].reshape(GROUP * CAP, 256), got[:, CAP:].reshape(GROUP * CAP, 256)], axis=1
@@ -570,10 +587,10 @@
             jax.ShapeDtypeStruct((ND, 2 * CAP, 256), BF16),
             jax.ShapeDtypeStruct((1, SLOTS), F32),
         ),
-        in_specs=[vmem, vmem, pl.BlockSpec(memory_space=pltpu.SMEM), hbm, hbm, hbm, hbm],
+        in_specs=[hbm, hbm, pl.BlockSpec(memory_space=pltpu.SMEM), hbm, hbm, hbm, hbm],
         out_specs=(vmem, vmem, vmem),
         scratch_shapes=[
-            V((ROWS, D), BF16), V((D, 4 * D), BF16), V((D, D), BF16), V((TOK, D), BF16), V((TOK, D), BF16), V((TOK, D), BF16),
+            V((1, TOK), jnp.int32), V((1, TOK), jnp.int32), V((ROWS, D), BF16), V((D, 4 * D), BF16), V((D, D), BF16), V((TOK, D), BF16), V((TOK, D), BF16), V((TOK, D), BF16),
             V((1, 1, TOK), jnp.int32), V((1, 1, TOK), jnp.int32), V((8, 1, ND), F32), V((8, 1, ND), F32), V((ND, 1, ND), F32),
             V((ND, 2 * CAP, 256), BF16), V((ND, 2 * CAP, 256), BF16), V((TOK, D), BF16),
             V((TOK, D), F32), V((TOK, 1), F32), V((TOK, 4 * D), F32), V((TOK, D), BF16), V((TOK, D), F32),
@@ -583,10 +600,10 @@
             V((NC, HD, TOK), BF16), V((NC, HD, TOK), BF16),
             V((TOK, HD), F32), V((2, HD, TOK), F32), V((TOK, D), F32), V((TOK, D), BF16),
             V((ND, 2 * CAP, 256), BF16),
-            DMA((4,)), DMA((3,)), DMA((3,)), DMA((2,)), DMA((2,)), DMA, DMA, DMA((9,)), DMA((9,)), DMA, DMA, DMA, DMA,
+            DMA((6,)), DMA((3,)), DMA((3,)), DMA((2,)), DMA((2,)), DMA, DMA, DMA((9,)), DMA((9,)), DMA, DMA, DMA, DMA,
         ],
         compiler_params=pltpu.CompilerParams(
-            collective_id=0, has_side_effects=True, vmem_limit_bytes=52 * 1024 * 1024
+            collective_id=0, has_side_effects=True, vmem_limit_bytes=63 * 1024 * 1024
         ),
     )(
         owner.reshape(1, TOK), row.reshape(1, TOK), lengths, table, proj_weight, out_weight,
@@ -597,13 +614,13 @@
         scatter_kernel,
         grid=(steps,),
         out_shape=(jax.ShapeDtypeStruct((ROWS, D), F32), jax.ShapeDtypeStruct((TOK, D), BF16)),
-        in_specs=[vmem, vmem, pl.BlockSpec((TOK // steps, D), lambda i: (i, 0))],
+        in_specs=[vmem, hbm, pl.BlockSpec((TOK // steps, D), lambda i: (i, 0))],
         out_specs=(
             pl.BlockSpec((ROWS // steps, D), lambda i: (i, 0)),
             pl.BlockSpec((TOK // steps, D), lambda i: (i, 0)),
         ),
-        scratch_shapes=[V((SLOTS, D), BF16)],
-        compiler_params=pltpu.CompilerParams(vmem_limit_bytes=32 * 1024 * 1024),
+        scratch_shapes=[V((SLOTS, D), BF16), V((ND, 2 * CAP, 256), BF16), DMA((ND // GROUP,))],
+        compiler_params=pltpu.CompilerParams(vmem_limit_bytes=63 * 1024 * 1024),
     )(wrow, recv2, mixed)
     return (mixed.reshape(1, TOK, D), table_grad)
 

time: 114 us -> 107 us (0.939)
  local copies, waits for them, and re-layouts: 4.66 us -> 0 us
  Pallas kernels: 107 us -> 105 us
    unnamed x10 -> x0, local copies, waits for them, and re-layouts: 4.66 us -> none
    pallas_call x1, Pallas kernels: 103 us -> 98.7 us  [shards(): pl.pallas_call(layer, out_shape=(jax.ShapeDtypeStruct((TOK, D), BF16), ja...]
    pallas_call x1, Pallas kernels: 4.15 us -> 6.59 us  [shards(): pl.pallas_call(scatter_kernel, grid=(steps,), out_shape=(jax.ShapeDtypeSt...]
where the time goes in v3:
time: 107 us
  Pallas kernels  105 us (98%)
  between operations  1.45 us (1%)
    pallas_call x1, Pallas kernels, shards(): pl.pallas_call(layer, out_shape=(jax.ShapeDtypeStruct((TOK, D), BF16), ja...  98.7 us
    pallas_call x1, Pallas kernels, shards(): pl.pallas_call(scatter_kernel, grid=(steps,), out_shape=(jax.ShapeDtypeSt...  6.59 us

profile of v3, /device:TPU:1, one launch (start us, length us, event | category | flops | bytes accessed | tf_op | source)
XLA Modules:
  0.0 106.7 jit_solution(7273376020012506903)
XLA Ops:
  1.3 98.7 %shard_map.86 = (bf16[512,512]{1,0:T(8,128)(2,1)}, bf16[128,16,256]{2,1,0:T(8,128)(2,1)}, f32[1,1024]{1,0:T(1,128)}) custom-call(s32[1,512]{1,0:T(1,128)} %bitcast.4, s32[1,512]{1,0:T(1,128)} %row_h.1, s32[1]{0:T(128)S(6)} %copy.9.length, bf16[2048,512]{1,0:T(8,128)(2,1)} %table_h.1, bf16[512,2048]{1,0:T(8,128)(2,1)} %pw_h.1, bf16[512,512]{1,0:T(8,128)(2,1)} %ow_h.1, ...), custom_call_target="tpu_custom_call" | custom-call | tf_op jit(solution)/shard_map/pallas_call | solution.py:583
  100.0 6.6 %shard_map.87 = (f32[2048,512]{1,0:T(8,128)}, bf16[512,512]{1,0:T(8,128)(2,1)}) custom-call(f32[1,1024]{1,0:T(1,128)} %get-tuple-element.7.wrow, bf16[128,16,256]{2,1,0:T(8,128)(2,1)} %get-tuple-element.8.recv2_h, bf16[512,512]{1,0:T(8,128)(2,1)} %get-tuple-element.9.mix), custom_call_target="tpu_custom_call" | custom-call | tf_op jit(solution)/shard_map/pallas_call | solution.py:613

commit v4 on v3

--- a/solution.py
+++ b/solution.py
@@ -471,7 +471,7 @@
     lax.fori_loop(1, NC, other_row, 0)
 
     def by_column(step, carry):
-        kb = rem(block + 1 + step, NC)
+        kb = rem(block + jnp.where(step < 2, 2 - step, step + 1), NC)
         d_kv[...] = jnp.zeros((2, HD, TOK), F32)
 
         def tile(qb, inner):

time: 107 us -> 105 us (0.981)
    pallas_call x1, Pallas kernels: 98.7 us -> 97.1 us  [shards(): pl.pallas_call(layer, out_shape=(jax.ShapeDtypeStruct((TOK, D), BF16), ja...]
where the time goes in v4:
time: 105 us
  Pallas kernels  104 us (99%)
  between operations  1.45 us (1%)
    pallas_call x1, Pallas kernels, shards(): pl.pallas_call(layer, out_shape=(jax.ShapeDtypeStruct((TOK, D), BF16), ja...  97.1 us
    pallas_call x1, Pallas kernels, shards(): pl.pallas_call(scatter_kernel, grid=(steps,), out_shape=(jax.ShapeDtypeSt...  6.59 us

profile of v4, /device:TPU:1, one launch (start us, length us, event | category | flops | bytes accessed | tf_op | source)
XLA Modules:
  0.0 105.2 jit_solution(7813576984228151048)
XLA Ops:
  1.3 97.1 %shard_map.86 = (bf16[512,512]{1,0:T(8,128)(2,1)}, bf16[128,16,256]{2,1,0:T(8,128)(2,1)}, f32[1,1024]{1,0:T(1,128)}) custom-call(s32[1,512]{1,0:T(1,128)} %bitcast.4, s32[1,512]{1,0:T(1,128)} %row_h.1, s32[1]{0:T(128)S(6)} %copy.9.length, bf16[2048,512]{1,0:T(8,128)(2,1)} %table_h.1, bf16[512,2048]{1,0:T(8,128)(2,1)} %pw_h.1, bf16[512,512]{1,0:T(8,128)(2,1)} %ow_h.1, ...), custom_call_target="tpu_custom_call" | custom-call | tf_op jit(solution)/shard_map/pallas_call | solution.py:583
  98.4 6.6 %shard_map.87 = (f32[2048,512]{1,0:T(8,128)}, bf16[512,512]{1,0:T(8,128)(2,1)}) custom-call(f32[1,1024]{1,0:T(1,128)} %get-tuple-element.7.wrow, bf16[128,16,256]{2,1,0:T(8,128)(2,1)} %get-tuple-element.8.recv2_h, bf16[512,512]{1,0:T(8,128)(2,1)} %get-tuple-element.9.mix), custom_call_target="tpu_custom_call" | custom-call | tf_op jit(solution)/shard_map/pallas_call | solution.py:613
